TPU v7x, 32 devices: a whole 2x2x4 slice. The times are simulated.
32 devices in a mesh: front: 2 (over core), row: 4 (over y, x), col: 4 (over z).
Axes of the slice: x: 2, y: 2, z: 4, core: 2. Of those that a mesh axis runs over, the one named last changes fastest.
Arguments:
- front_matrix: bfloat16 [2, 6, 4, 256, 6, 4, 256], P('front', None, 'row', None, None, 'col'), as said below
- contributions: bfloat16 [2, 4, 4, 32, 256, 256], P('front', 'row', 'col'), may hold values from -3 to 3
- target_front: int32 [2, 4, 4, 32], P('front', 'row', 'col'), may hold values from 0 to 1, as said below
- target_row: int32 [2, 4, 4, 32], P('front', 'row', 'col'), may hold values from 4 to 23, as said below
- target_col: int32 [2, 4, 4, 32], P('front', 'row', 'col'), may hold values from 0 to 22, as said below
- live_count: int32 [2, 4, 4], P('front', 'row', 'col'), may hold values from 24 to 32
Outputs:
- factor: float32 [2, 6, 4, 256, 6, 4, 256], P('front', None, 'row', None, None, 'col')
Inputs may be any that keep to these rules, and one draw needn't show every extreme that they name: `front_matrix`: Symmetric; its leading 2 * 2 * 256 rows and columns form a strictly diagonally dominant block with a positive diagonal. `target_front`: among one device's live slots at most 4 aim at one pair of parent front and target_row modulo the number of row devices, and on every device one such pair takes exactly 4. `target_row`: never one of the first 4 tile rows, nor one of the first tile rows as many as the col devices. `target_col`: below the slot's target_row, and congruent to the holding device's col index modulo the number of col devices.
All inputs are finite; a program needn't handle non-finite values.
Results may differ from a plain program's by a relative error of at most 0.0003.
Values may be sent and summed in bfloat16 or wider, within the bound.
A program may use at most 128 MiB of HBM per device.

v0:
```python
import jax
import jax.numpy as jnp
import numpy as np
from jax import lax
from jax.sharding import PartitionSpec as P

PANEL_TILES = 2
PANELS = 2


def broadcast(array, axis, root):
    mine = lax.axis_index(axis) == root
    return lax.psum(jnp.where(mine, array, jnp.zeros_like(array)), axis)


def mirror_tiles(square, tile_size):
    tile_ids = jnp.arange(square.shape[0]) // tile_size
    return jnp.where(tile_ids[:, None] >= tile_ids[None, :], square, square.T)


def panel_factor(square, tile_size):
    return jnp.linalg.cholesky(mirror_tiles(square, tile_size))


def below_solve(lead_factor, row_block):
    return lax.linalg.triangular_solve(
        lead_factor, row_block, left_side=False, lower=True, transpose_a=True
    )


def pack_buckets(
    contrib_tiles, destination, live_slots, slot_ids, bucket_total, capacity, local_tile
):
    earlier = (
        (destination[:, None] == destination[None, :])
        & live_slots[None, :]
        & (slot_ids[None, :] < slot_ids[:, None])
    )
    position = jnp.sum(earlier.astype(jnp.int32), axis=1)
    bucket = destination * capacity + position
    matches = (bucket[None, :] == jnp.arange(bucket_total, dtype=jnp.int32)[:, None]) & live_slots[
        None, :
    ]
    source = jnp.sum(jnp.where(matches, slot_ids[None, :], 0), axis=1)
    filled = jnp.any(matches, axis=1)
    packed = jnp.where(filled[:, None, None], contrib_tiles[source], jnp.zeros((), jnp.bfloat16))
    targets = jnp.where(filled, local_tile[source], -1)
    return (packed, targets)


def route_tiles(
    contributions,
    target_front,
    target_row,
    target_col,
    live_count,
    tile_cols,
    n_front,
    n_row,
    n_col,
):
    slot_total = contributions.shape[3]
    tile_size = contributions.shape[4]
    contrib_tiles = contributions.reshape(slot_total, tile_size, tile_size)
    fronts_to = target_front.reshape(slot_total)
    rows_to = target_row.reshape(slot_total)
    cols_to = target_col.reshape(slot_total)
    slot_ids = jnp.arange(slot_total, dtype=jnp.int32)
    live_slots = slot_ids < live_count.reshape(())
    capacity = max(2, -(-slot_total // (n_front * n_row)))
    local_tile = rows_to // n_row * tile_cols + cols_to // n_col
    destination = fronts_to * n_row + rows_to % n_row
    bucket_total = n_front * n_row * capacity
    packed, targets = pack_buckets(
        contrib_tiles, destination, live_slots, slot_ids, bucket_total, capacity, local_tile
    )
    received, arrived = (
        lax.all_to_all(packed, ("front", "row"), split_axis=0, concat_axis=0, tiled=True),
        lax.all_to_all(targets, ("front", "row"), split_axis=0, concat_axis=0, tiled=True),
    )
    return (received, arrived)


def per_device(front_matrix, contributions, target_front, target_row, target_col, live_count):
    tile_rows = front_matrix.shape[1]
    tile_size = front_matrix.shape[3]
    tile_cols = front_matrix.shape[4]
    n_front = lax.axis_size("front")
    n_row = lax.axis_size("row")
    n_col = lax.axis_size("col")
    row_index = lax.axis_index("row")
    col_index = lax.axis_index("col")
    work = front_matrix.reshape(tile_rows, tile_size, tile_cols, tile_size).astype(jnp.float32)
    received, arrived = route_tiles(
        contributions,
        target_front,
        target_row,
        target_col,
        live_count,
        tile_cols,
        n_front,
        n_row,
        n_col,
    )
    local_total = tile_rows * tile_cols
    selector = (arrived[None, :] == jnp.arange(local_total, dtype=jnp.int32)[:, None]).astype(
        jnp.bfloat16
    )
    assembled = jnp.dot(
        selector,
        received.reshape(received.shape[0], tile_size * tile_size),
        preferred_element_type=jnp.float32,
    )
    work = work + assembled.reshape(tile_rows, tile_cols, tile_size, tile_size).transpose(
        0, 2, 1, 3
    )
    global_rows = jnp.arange(tile_rows, dtype=jnp.int32) * n_row + row_index
    global_cols = jnp.arange(tile_cols, dtype=jnp.int32) * n_col + col_index
    panel_width = PANEL_TILES * tile_size
    for panel_number in range(PANELS):
        first_tile = panel_number * PANEL_TILES
        after_tile = first_tile + PANEL_TILES
        pieces = []
        for member in range(PANEL_TILES):
            tile_index = first_tile + member
            pieces.append(broadcast(work[:, :, tile_index // n_col, :], "col", tile_index % n_col))
        rows_panel = jnp.concatenate(pieces, axis=2)
        diagonal_part = jnp.stack(
            [
                jnp.where(
                    row_index == (first_tile + member) % n_row,
                    rows_panel[(first_tile + member) // n_row],
                    0.0,
                )
                for member in range(PANEL_TILES)
            ]
        )
        lead_block = (
            lax.psum(diagonal_part.astype(jnp.bfloat16), "row")
            .astype(jnp.float32)
            .reshape(panel_width, panel_width)
        )
        lead_factor = panel_factor(lead_block, tile_size)
        solved = below_solve(
            lead_factor, rows_panel.reshape(tile_rows * tile_size, panel_width)
        ).reshape(tile_rows, tile_size, panel_width)
        offset = global_rows - first_tile
        in_panel = (offset >= 0) & (offset < PANEL_TILES)
        picked = lead_factor.reshape(PANEL_TILES, tile_size, panel_width)[
            jnp.clip(offset, 0, PANEL_TILES - 1)
        ]
        row_mask = global_rows >= after_tile
        factor_rows = jnp.where(
            row_mask[:, None, None], solved, jnp.where(in_panel[:, None, None], picked, 0.0)
        )
        grouped = factor_rows.reshape(tile_cols, n_col // n_row, tile_size, panel_width)
        own_piece = lax.dynamic_index_in_dim(grouped, col_index // n_row, axis=1, keepdims=False)
        cols_panel = broadcast(own_piece, "row", col_index % n_row)
        col_mask = global_cols >= after_tile
        for member in range(PANEL_TILES):
            tile_index = first_tile + member
            local_col = tile_index // n_col
            owner = col_index == tile_index % n_col
            stored = jnp.where(
                owner,
                factor_rows[:, :, member * tile_size : (member + 1) * tile_size],
                work[:, :, local_col, :],
            )
            work = work.at[:, :, local_col, :].set(stored)
        early_slots = []
        late_slots = [
            slot_number for slot_number in range(tile_cols) if slot_number not in early_slots
        ]
        for group_slots in (early_slots, late_slots):
            if group_slots:
                indices = np.array(group_slots, dtype=np.int32)
                update = jnp.einsum(
                    "atk,bsk->atbs",
                    factor_rows,
                    cols_panel[indices],
                    precision=lax.Precision.HIGHEST,
                    preferred_element_type=jnp.float32,
                )
                trailing_mask = (
                    row_mask[:, None, None, None] & col_mask[indices][None, None, :, None]
                )
                work = work.at[:, :, indices, :].add(-jnp.where(trailing_mask, update, 0.0))
    lower = global_rows[:, None] >= global_cols[None, :]
    factor = jnp.where(lower[:, None, :, None], work, 0.0)
    return factor.reshape(1, tile_rows, 1, tile_size, tile_cols, 1, tile_size)


def solution(mesh):
    in_specs = (
        P("front", None, "row", None, None, "col", None),
        P("front", "row", "col", None, None, None),
        P("front", "row", "col", None),
        P("front", "row", "col", None),
        P("front", "row", "col", None),
        P("front", "row", "col"),
    )
    out_specs = P("front", None, "row", None, None, "col", None)
    return jax.shard_map(
        per_device, mesh=mesh, in_specs=in_specs, out_specs=out_specs, check_vma=False
    )
```

profile of v0, /device:TPU:2, one launch (start us, length us, event | category | flops | bytes accessed | tf_op | source)
XLA Modules:
  0.0 1063.2 jit_solution(7094981757221635369)
XLA Ops:
  29.4 46.3 %all-to-all-done.1 = bf16[32,256,256]{2,1,0:T(8,128)(2,1)} async-done(((bf16[32,256,256]{2,1,0:T(8,128)(2,1)}), bf16[32,256,256]{2,1,0:T(8,128)(2,1)}, u32[]{:S(2)}, u32[]{:S(2)}) %all-to-all-start.1) | async-done | bytes 4194336 | tf_op jit(solution)/shard_map/all_to_all | solution.py:78
  93.8 121.9 %all-reduce.20.cloned.1.call-done = (f32[6,256,256]{2,1,0:T(8,128)}, f32[6,256,256]{2,1,0:T(8,128)}) async-done(((f32[6,256,256]{2,1,0:T(8,128)}, f32[6,256,256]{2,1,0:T(8,128)}), (f32[6,256,256]{2,1,0:T(8,128)}, f32[6,256,256]{2,1,0:T(8,128)})) %all-reduce.20.cloned.1.call-update) | async-done | bytes 3145744 | tf_op jit(solution)/shard_map/psum | solution.py:13
  220.8 44.2 %all-reduce.10.cloned.1.call-done = bf16[512,512]{1,0:T(8,128)(2,1)} async-done(((bf16[512,512]{1,0:T(8,128)(2,1)}), bf16[512,512]{1,0:T(8,128)(2,1)}) %all-reduce.10.cloned.1.call-update) | async-done | bytes 524304 | tf_op jit(solution)/shard_map/psum | solution.py:139
  268.0 11.7 %cholesky.286 = f32[128,128]{1,0:T(8,128)S(1)} custom-call(f32[128,128]{1,0:T(8,128)S(1)} %cholesky.426), custom_call_target="Cholesky" | custom-call | tf_op jit(solution)/shard_map/jit(cholesky)/cholesky | solution.py:22
  290.4 11.7 %cholesky.305 = f32[128,128]{1,0:T(8,128)S(1)} custom-call(f32[128,128]{1,0:T(8,128)S(1)} %cholesky.430), custom_call_target="Cholesky" | custom-call | tf_op jit(solution)/shard_map/jit(cholesky)/cholesky | solution.py:22
  313.1 11.7 %cholesky.326 = f32[128,128]{1,0:T(8,128)S(1)} custom-call(f32[128,128]{1,0:T(8,128)S(1)} %cholesky.435), custom_call_target="Cholesky" | custom-call | tf_op jit(solution)/shard_map/jit(cholesky)/cholesky | solution.py:22
  335.2 11.9 %cholesky.343 = f32[128,128]{1,0:T(8,128)S(1)} custom-call(f32[128,128]{1,0:T(8,128)S(1)} %convolution_subtract_fusion.11), custom_call_target="Cholesky" | custom-call | tf_op jit(solution)/shard_map/jit(cholesky)/cholesky | solution.py:22
  361.0 39.3 %custom-call.30 = f32[4,128,128]{1,2,0:T(8,128)S(1)} custom-call(f32[4,128,128]{2,1,0:T(8,128)S(1)} %get-tuple-element.69), custom_call_target="InvertDiagBlocksLowerTriangular" | custom-call | tf_op jit(solution)/shard_map/triangular_solve/custom-call.3 | solution.py:26
  434.8 36.0 %scatter.14 = f32[6,256,6,256]{3,2,1,0:T(8,128)} dynamic-update-slice(f32[6,256,6,256]{3,2,1,0:T(8,128)} %copy-done, f32[6,256,1,256]{3,2,1,0:T(1,128)} %copy.73, s32[]{:T(128)} %copy.156, s32[]{:T(128)} %copy.156, s32[]{:T(128)} %copy.156, s32[]{:T(128)} %copy.156) | dynamic-update-slice | bytes 3145732 | tf_op jit(solution)/shard_map/scatter | solution.py:169
  474.5 36.2 %scatter.15 = f32[6,256,6,256]{3,2,1,0:T(8,128)} dynamic-update-slice(f32[6,256,6,256]{3,2,1,0:T(8,128)} %scatter.14, f32[6,256,1,256]{3,2,1,0:T(1,128)} %reshape.562, s32[]{:T(128)} %copy.156, s32[]{:T(128)} %copy.156, s32[]{:T(128)} %copy.156, s32[]{:T(128)} %copy.156) | dynamic-update-slice | bytes 3145732 | tf_op jit(solution)/shard_map/scatter | solution.py:169
  510.6 11.2 %copy.74 = f32[6,256,6,256]{3,1,2,0:T(8,128)} copy(f32[6,256,6,256]{3,2,1,0:T(8,128)} %scatter.15) | data formatting | bytes 18874368 | tf_op jit(solution)/shard_map/scatter | solution.py:169
  526.2 18.4 %negate_bitcast_fusion.1 = f32[6,6,256,256]{3,2,0,1:T(8,128)S(1)} fusion(pred[6,6]{1,0:T(8,128)(4,1)S(1)} %broadcast_and_fusion.1, f32[6,256,512]{2,1,0:T(8,128)S(1)} %get-tuple-element.96, f32[6,256,512]{2,1,0:T(8,128)} %gather_fusion.4), kind=kOutput, calls=%fused_computation.17 | convolution fusion | flops 14500233216 | bytes 15728676 | tf_op jit(solution)/shard_map/atk,bsk->atbs/dot_general | solution.py:177
  549.3 19.6 %scatter_fusion = f32[6,256,6,256]{3,1,2,0:T(8,128)} fusion(f32[6,256,6,256]{3,1,2,0:T(8,128)} %copy.74, s32[6]{0:T(128)S(1)} %iota.131, f32[6,6,256,256]{3,2,1,0:T(8,128)} %copy.75), kind=kCustom, calls=%fused_computation.8 | custom fusion | flops 2359296 | bytes 28311576 | tf_op jit(solution)/shard_map/scatter-add | solution.py:187
  572.4 121.6 %all-reduce.18.cloned.1.call-done = (f32[6,256,256]{2,1,0:T(8,128)}, f32[6,256,256]{2,1,0:T(8,128)}) async-done(((f32[6,256,256]{2,1,0:T(8,128)}, f32[6,256,256]{2,1,0:T(8,128)}), (f32[6,256,256]{2,1,0:T(8,128)}, f32[6,256,256]{2,1,0:T(8,128)})) %all-reduce.18.cloned.1.call-update) | async-done | bytes 3145744 | tf_op jit(solution)/shard_map/psum | solution.py:13
  699.0 44.2 %all-reduce.14.cloned.1.call-done = bf16[512,512]{1,0:T(8,128)(2,1)} async-done(((bf16[512,512]{1,0:T(8,128)(2,1)}), bf16[512,512]{1,0:T(8,128)(2,1)}) %all-reduce.14.cloned.1.call-update) | async-done | bytes 524304 | tf_op jit(solution)/shard_map/psum | solution.py:139
  746.3 11.7 %cholesky.358 = f32[128,128]{1,0:T(8,128)S(1)} custom-call(f32[128,128]{1,0:T(8,128)S(1)} %cholesky.439), custom_call_target="Cholesky" | custom-call | tf_op jit(solution)/shard_map/jit(cholesky)/cholesky | solution.py:22
  768.7 11.7 %cholesky.377 = f32[128,128]{1,0:T(8,128)S(1)} custom-call(f32[128,128]{1,0:T(8,128)S(1)} %cholesky.443), custom_call_target="Cholesky" | custom-call | tf_op jit(solution)/shard_map/jit(cholesky)/cholesky | solution.py:22
  791.4 11.7 %cholesky.398 = f32[128,128]{1,0:T(8,128)S(1)} custom-call(f32[128,128]{1,0:T(8,128)S(1)} %cholesky.448), custom_call_target="Cholesky" | custom-call | tf_op jit(solution)/shard_map/jit(cholesky)/cholesky | solution.py:22
  813.5 11.9 %cholesky.415 = f32[128,128]{1,0:T(8,128)S(1)} custom-call(f32[128,128]{1,0:T(8,128)S(1)} %convolution_subtract_fusion.10), custom_call_target="Cholesky" | custom-call | tf_op jit(solution)/shard_map/jit(cholesky)/cholesky | solution.py:22
  838.3 39.3 %custom-call.34 = f32[4,128,128]{1,2,0:T(8,128)S(1)} custom-call(f32[4,128,128]{2,1,0:T(8,128)S(1)} %get-tuple-element.70), custom_call_target="InvertDiagBlocksLowerTriangular" | custom-call | tf_op jit(solution)/shard_map/triangular_solve/custom-call.3 | solution.py:26
  910.6 82.1 %all-reduce.16.cloned.1.call-done = f32[6,256,512]{2,1,0:T(8,128)} async-done(((f32[6,256,512]{2,1,0:T(8,128)}), f32[6,256,512]{2,1,0:T(8,128)}) %all-reduce.16.cloned.1.call-update) | async-done | bytes 3145744 | tf_op jit(solution)/shard_map/psum | solution.py:13
  997.0 18.5 %negate_bitcast_fusion = f32[6,6,256,256]{3,2,0,1:T(8,128)S(1)} fusion(pred[6,6]{1,0:T(8,128)(4,1)S(1)} %broadcast_and_fusion, f32[6,256,512]{2,1,0:T(8,128)S(1)} %get-tuple-element.92, f32[6,256,512]{2,1,0:T(8,128)} %gather_fusion.7), kind=kOutput, calls=%fused_computation.16 | convolution fusion | flops 14500233216 | bytes 15728676 | tf_op jit(solution)/shard_map/atk,bsk->atbs/dot_general | solution.py:177
  1020.2 19.6 %scatter_fusion.1 = f32[6,256,6,256]{3,1,2,0:T(8,128)} fusion(f32[6,256,6,256]{3,1,2,0:T(8,128)} %fusion.22, s32[6]{0:T(128)S(1)} %iota.134, f32[6,6,256,256]{3,2,1,0:T(8,128)} %copy.82), kind=kCustom, calls=%fused_computation.9 | custom fusion | flops 2359296 | bytes 28311576 | tf_op jit(solution)/shard_map/scatter-add | solution.py:187
  1044.8 11.1 %copy.83 = f32[1,6,1,256,6,1,256]{6,5,4,3,2,1,0:T(1,128)} copy(f32[1,6,1,256,6,1,256]{6,3,4,1,5,2,0:T(8,128)S(1)} %select_bitcast_fusion) | data formatting | bytes 18874368 | tf_op jit(solution)/shard_map/reshape | solution.py:190
  (192 shorter events, 255.3 us)
Async XLA Ops:
  9.7 13.8 %all-to-all-start = ((s32[8,4,1]{1,2,0:T(1,128)}), s32[8,4,1]{1,2,0:T(1,128)S(1)}, u32[]{:S(2)}, u32[]{:S(2)}) async-start(s32[8,4,1]{1,2,0:T(1,128)} %bitcast.7), calls=%async_computation | async-start | bytes 8192 | tf_op jit(solution)/shard_map/all_to_all | solution.py:79
  23.6 52.1 %all-to-all-start.1 = ((bf16[32,256,256]{2,1,0:T(8,128)(2,1)}), bf16[32,256,256]{2,1,0:T(8,128)(2,1)}, u32[]{:S(2)}, u32[]{:S(2)}) async-start(bf16[32,256,256]{2,1,0:T(8,128)(2,1)} %broadcast_select_fusion), calls=%async_computation.1 | async-start | bytes 8388608 | tf_op jit(solution)/shard_map/all_to_all | solution.py:78
  28.1 187.6 %all-reduce.20.cloned.1.call-start = ((), (), s32[]{:S(2)}) async-start(), calls=%async_computation.7 | async-start | bytes 6291456 | tf_op jit(solution)/shard_map/psum | solution.py:13
  85.0 4.6 copy-start
  90.6 1.2 copy-start.1
  93.7 171.2 %all-reduce.10.cloned.1.call-start = ((), (), s32[]{:S(2)}) async-start(), calls=%async_computation.2 | async-start | bytes 1048576 | tf_op jit(solution)/shard_map/psum | solution.py:139
  215.7 1.9 copy-start.6
  217.8 1.7 copy-start.2
  220.5 301.4 %all-reduce.12.cloned.1.call-start = ((), (), s32[]{:S(2)}) async-start(), calls=%async_computation.3 | async-start | bytes 6291456 | tf_op jit(solution)/shard_map/psum | solution.py:13
  400.3 5.6 copy-start.3
  428.1 265.9 %all-reduce.18.cloned.1.call-start = ((), (), s32[]{:S(2)}) async-start(), calls=%async_computation.6 | async-start | bytes 6291456 | tf_op jit(solution)/shard_map/psum | solution.py:13
  572.4 170.9 %all-reduce.14.cloned.1.call-start = ((), (), s32[]{:S(2)}) async-start(), calls=%async_computation.4 | async-start | bytes 1048576 | tf_op jit(solution)/shard_map/psum | solution.py:139
  694.0 1.9 copy-start.7
  696.1 1.7 copy-start.4
  698.8 293.9 %all-reduce.16.cloned.1.call-start = ((), (), s32[]{:S(2)}) async-start(), calls=%async_computation.5 | async-start | bytes 6291456 | tf_op jit(solution)/shard_map/psum | solution.py:13
  877.6 5.6 copy-start.5
Sparse Core Ops, SparseCore 0:
  93.9 121.7 all-reduce.19
  220.6 44.3 all-reduce.9
  428.3 87.1 all-reduce.11
  572.5 121.4 all-reduce.17
  698.9 44.3 all-reduce.13
  905.4 87.1 all-reduce.15
where the time goes:
time: 1070 us; the launch traced here: 1060 us
  waiting for transfers between devices  460 us (43%)
  other arithmetic  320 us (30%)
  local copies, waits for them, and re-layouts  175 us (16%)
  matrix products  77.9 us (7%)
  between operations  20.5 us (2%)
    psum x4, waiting for transfers between devices, broadcast(): return lax.psum(jnp.where(mine, array, jnp.zeros_like(array)), axis)  326 us
    another operation x29, other arithmetic, panel_factor(): return jnp.linalg.cholesky(mirror_tiles(square, tile_size))  159 us
    psum x2, waiting for transfers between devices, per_device(): lax.psum(diagonal_part.astype(jnp.bfloat16), 'row').astype(jnp.float32)  88.4 us
    scatter x4, local copies, waits for them, and re-layouts, per_device(): work = work.at[:, :, local_col, :].set(stored)  84.7 us
    another operation x7, other arithmetic, below_solve(): lax.linalg.triangular_solve(lead_factor, row_block, left_side=False, lowe...  82.9 us
    all_to_all x1, waiting for transfers between devices, route_tiles(): lax.all_to_all(packed, ('front', 'row'), split_axis=0, concat_axis=0, til...  46.3 us
    scatter-add x2, other arithmetic, per_device(): work = work.at[:, :, indices, :].add(-jnp.where(trailing_mask, update, 0.0))  39.2 us
    dot_general x2, matrix products, per_device(): jnp.einsum('atk,bsk->atbs', factor_rows, cols_panel[indices], precision=l...  36.9 us
  transfers between devices with their start and end apart: 8, of which 6 were waited for; matrix products, arithmetic and copies ran while one was open for 10% of the time, Pallas kernels for 0%

commit v1 on v0

v1 whole, which is shorter than its diff:
```python
import functools

import jax
import jax.numpy as jnp
from jax import lax
from jax.experimental import pallas as pl
from jax.experimental.pallas import tpu as pltpu
from jax.sharding import PartitionSpec as P

PANEL_TILES = 2
PANELS = 2
LEAD = PANEL_TILES * PANELS
BLOCK = 128
HIGHEST = lax.Precision.HIGHEST
NT = (((1,), (1,)), ((), ()))
F32 = jnp.float32
BF16 = jnp.bfloat16


def mm(a, b):
    return jnp.dot(a, b, precision=HIGHEST, preferred_element_type=F32)


def mm_nt(a, b):
    return lax.dot_general(a, b, NT, precision=HIGHEST, preferred_element_type=F32)


def split(x):
    hi = x.astype(BF16)
    return hi, (x - hi.astype(F32)).astype(BF16)


def mm3_nt(a, b):
    (ah, al), (bh, bl) = a, b
    one = functools.partial(lax.dot_general, dimension_numbers=NT, preferred_element_type=F32)
    return one(ah, bh) + (one(ah, bl) + one(al, bh))


def eliminate(block):
    groups = BLOCK // 8
    upper = [block[8 * i : 8 * i + 8, :] for i in range(groups)]
    rows = lax.broadcasted_iota(jnp.int32, (8, BLOCK), 0)
    lanes = lax.broadcasted_iota(jnp.int32, (8, BLOCK), 1)
    inverse = [jnp.where(rows + 8 * i == lanes, 1.0, 0.0).astype(F32) for i in range(groups)]
    sub = lax.broadcasted_iota(jnp.int32, (8, 1), 0)
    for j in range(BLOCK):
        g, s = divmod(j, 8)
        row_u = upper[g][s : s + 1, :]
        row_i = inverse[g][s : s + 1, :]
        scale = 1.0 / row_u[:, j : j + 1]
        row_u = row_u * scale
        row_i = row_i * scale
        for i in range(g, groups):
            column = upper[i][:, j : j + 1]
            if i == g:
                if s == 7:
                    continue
                column = jnp.where(sub > s, column, 0.0)
            upper[i] = upper[i] - column * row_u
            inverse[i] = inverse[i] - column * row_i
    return jnp.concatenate(upper, axis=0), jnp.concatenate(inverse, axis=0)


def factor_panel(work, lower, inverse, base):
    size = work.shape[0]
    ids = lax.broadcasted_iota(jnp.int32, (size, size), 0)
    inverse[...] = jnp.where(
        ids == lax.broadcasted_iota(jnp.int32, (size, size), 1), 1.0, 0.0
    ).astype(F32)
    row_ids = lax.broadcasted_iota(jnp.int32, (size, BLOCK), 0)
    eye = lax.broadcasted_iota(jnp.int32, (BLOCK, BLOCK), 0) == lax.broadcasted_iota(
        jnp.int32, (BLOCK, BLOCK), 1
    )
    above = lax.broadcasted_iota(jnp.int32, (BLOCK, BLOCK), 0) <= lax.broadcasted_iota(
        jnp.int32, (BLOCK, BLOCK), 1
    )

    def step(k, carry):
        start = pl.multiple_of(k * BLOCK, BLOCK)
        here = pl.ds(start, BLOCK)
        upper, unit = eliminate(work[here, here])
        diagonal = jnp.sum(jnp.where(eye, upper, 0.0), axis=1, keepdims=True)
        root = lax.rsqrt(diagonal)
        root = root * (1.5 - 0.5 * diagonal * root * root)
        small = unit * root
        column = mm_nt(work[:, here], small)
        below = jnp.where(row_ids >= start + BLOCK, column, 0.0)
        lower[pl.ds(base, size), pl.ds(pl.multiple_of(base + start, BLOCK), BLOCK)] = below
        lower[
            pl.ds(pl.multiple_of(base + start, BLOCK), BLOCK),
            pl.ds(pl.multiple_of(base + start, BLOCK), BLOCK),
        ] = jnp.where(above, upper * root, 0.0).T
        solved = mm(small, inverse[here, :])
        inverse[here, :] = solved
        work[...] -= mm_nt(below, below)
        inverse[...] -= mm(below, solved)
        return carry

    lax.fori_loop(0, size // BLOCK, step, 0)


def load_square(lead, work, row0, col0, tile):
    for i in range(PANEL_TILES):
        for j in range(PANEL_TILES):
            work[i * tile : (i + 1) * tile, j * tile : (j + 1) * tile] = lead[
                row0 + i, col0 + j
            ].astype(F32)


def first_kernel(tile, lead, lower, inverse, work):
    load_square(lead, work, 0, 0, tile)
    factor_panel(work, lower, inverse, 0)


def second_kernel(tile, n_row, n_col, spot, lead, lower0, inverse0, high, low, own, work, lower, inverse):
    width = PANEL_TILES * tile
    load_square(lead, work, PANEL_TILES, 0, tile)
    left = mm_nt(work[...], inverse0[...])
    load_square(lead, work, PANEL_TILES, PANEL_TILES, tile)
    work[...] -= mm_nt(left, left)
    lower[:width, :width] = lower0[...]
    lower[:width, width:] = jnp.zeros((width, width), F32)
    lower[width:, :width] = left
    factor_panel(work, lower, inverse, width)
    corner = -mm(inverse[...], mm(left, inverse0[...]))
    for r, c, value in (
        (0, 0, inverse0[...]),
        (0, 1, jnp.zeros((width, width), F32)),
        (1, 0, corner),
        (1, 1, inverse[...]),
    ):
        hi, lo = split(value)
        high[r * width : (r + 1) * width, c * width : (c + 1) * width] = hi
        low[r * width : (r + 1) * width, c * width : (c + 1) * width] = lo
    own[...] = lower[
        pl.ds(pl.multiple_of(jnp.minimum(spot[0], LEAD - 1) * tile, tile), tile),
        pl.ds(pl.multiple_of(jnp.minimum(spot[1], LEAD - 1) * tile, tile), tile),
    ]


def whole(space=pltpu.VMEM):
    return pl.BlockSpec(memory_space=space)


def estimate(us, size):
    return pl.CostEstimate(flops=int(us * 1e9), bytes_accessed=size, transcendentals=0)


def lead_factor(lead, spot, tile, n_row, n_col):
    width = PANEL_TILES * tile
    square = jax.ShapeDtypeStruct((width, width), F32)
    params = pltpu.CompilerParams(vmem_limit_bytes=48 << 20)
    lower0, inverse0 = pl.pallas_call(
        functools.partial(first_kernel, tile),
        out_shape=(square, square),
        in_specs=[whole()],
        out_specs=(whole(), whole()),
        scratch_shapes=[pltpu.VMEM((width, width), F32)],
        compiler_params=params,
        cost_estimate=estimate(60, 1 << 20),
        name="lead_first",
    )(lead)
    full = (2 * width, 2 * width)
    high, low, own = pl.pallas_call(
        functools.partial(second_kernel, tile, n_row, n_col),
        out_shape=(
            jax.ShapeDtypeStruct(full, BF16),
            jax.ShapeDtypeStruct(full, BF16),
            jax.ShapeDtypeStruct((tile, tile), F32),
        ),
        in_specs=[whole(pltpu.SMEM)] + [whole()] * 3,
        out_specs=(whole(),) * 3,
        scratch_shapes=[
            pltpu.VMEM((width, width), F32),
            pltpu.VMEM(full, F32),
            pltpu.VMEM((width, width), F32),
        ],
        compiler_params=params,
        cost_estimate=estimate(60, 1 << 20),
        name="lead_second",
    )(spot, lead, lower0, inverse0)
    return high, low, own


def pack_kernel(count, capacity, source, tiles, *rest):
    buckets, sems = rest[:count], rest[count]
    copies = []
    for k in range(count):
        for p in range(capacity):
            n = k * capacity + p
            copies.append(
                pltpu.make_async_copy(tiles.at[source[n]], buckets[k].at[p], sems.at[n])
            )
    for copy in copies:
        copy.start()
    for copy in copies:
        copy.wait()


def route_tiles(contributions, target_front, target_row, target_col, live_count, tile_cols, n_front, n_row, n_col):
    slots = contributions.shape[3]
    tile = contributions.shape[4]
    tiles = contributions.reshape(slots, tile, tile)
    fronts_to = target_front.reshape(slots)
    rows_to = target_row.reshape(slots)
    cols_to = target_col.reshape(slots)
    ids = jnp.arange(slots, dtype=jnp.int32)
    live = ids < live_count.reshape(())
    count = n_front * n_row
    capacity = max(2, -(-slots // count))
    me = lax.axis_index("front") * n_row + lax.axis_index("row")
    local_tile = rows_to // n_row * tile_cols + cols_to // n_col
    bucket_of = jnp.bitwise_xor(fronts_to * n_row + rows_to % n_row, me)
    earlier = (bucket_of[:, None] == bucket_of[None, :]) & live[None, :] & (ids[None, :] < ids[:, None])
    place = bucket_of * capacity + jnp.sum(earlier.astype(jnp.int32), axis=1)
    matches = (place[None, :] == jnp.arange(count * capacity, dtype=jnp.int32)[:, None]) & live[None, :]
    source = jnp.sum(jnp.where(matches, ids[None, :], 0), axis=1)
    filled = jnp.any(matches, axis=1)
    targets = jnp.sum(jnp.where(matches, local_tile[None, :], 0), axis=1)
    targets = jnp.where(filled, targets, -1)
    buckets = pl.pallas_call(
        functools.partial(pack_kernel, count, capacity),
        out_shape=tuple(jax.ShapeDtypeStruct((capacity, tile, tile), BF16) for _ in range(count)),
        in_specs=[whole(pltpu.SMEM), whole(pl.ANY)],
        out_specs=tuple(whole(pl.ANY) for _ in range(count)),
        scratch_shapes=[pltpu.SemaphoreType.DMA((count * capacity,))],
        name="pack",
    )(source, tiles)
    axes = ("front", "row")
    received = [buckets[0]]
    for k in range(1, count):
        received.append(lax.ppermute(buckets[k], axes, [(i, i ^ k) for i in range(count)]))
    everyone = lax.all_gather(targets.reshape(count, capacity), axes)
    everyone = everyone.reshape(count, count, capacity)
    arrived = jnp.stack(
        [everyone[jnp.bitwise_xor(me, k), k] for k in range(count)]
    ).reshape(-1)
    return received, arrived


def extend_kernel(count, capacity, tile_cols, tile, arrived, front, *rest):
    received, out = rest[:count], rest[count]
    row = pl.program_id(0)
    out[...] = front[...].astype(F32)
    for k in range(count):
        for p in range(capacity):
            target = arrived[k * capacity + p]

            @pl.when((target >= 0) & (target // tile_cols == row))
            def _():
                column = pl.multiple_of(target % tile_cols * tile, tile)
                out[:, pl.ds(column, tile)] += received[k][p].astype(F32)


def extend(front, received, arrived, tile_rows, tile_cols, tile):
    count, capacity = len(received), received[0].shape[0]
    rows, cols = front.shape
    return pl.pallas_call(
        functools.partial(extend_kernel, count, capacity, tile_cols, tile),
        out_shape=jax.ShapeDtypeStruct((rows, cols), F32),
        grid=(tile_rows,),
        in_specs=[whole(pltpu.SMEM), pl.BlockSpec((tile, cols), lambda a: (a, 0))] + [whole()] * count,
        out_specs=pl.BlockSpec((tile, cols), lambda a: (a, 0)),
        compiler_params=pltpu.CompilerParams(vmem_limit_bytes=48 << 20),
        cost_estimate=estimate(8, rows * cols * 6),
        name="extend",
    )(arrived, front, *received)


def solve_rows(gathered, start, high, low, tile):
    parts = [split(gathered[c, pl.ds(start, tile), :]) for c in range(LEAD)]
    solved = []
    for n in range(LEAD):
        total = None
        for c in range(n + 1):
            rows = slice(n * tile, (n + 1) * tile)
            cols = slice(c * tile, (c + 1) * tile)
            term = mm3_nt(parts[c], (high[rows, cols], low[rows, cols]))
            total = term if total is None else total + term
        solved.append(total)
    return solved


def trailing_kernel(
    tile, n_row, n_col, tile_cols, row0, col0, spot, work, by_row, by_col, high, low, own, out, cols_hi, cols_lo, rows_f
):
    a = pl.program_id(0)
    row_index, col_index = spot[0], spot[1]

    @pl.when(a == 0)
    def _():
        def body(b, carry):
            start = pl.multiple_of(b * tile, tile)
            solved = solve_rows(by_col, start, high, low, tile)
            for n in range(LEAD):
                hi, lo = split(solved[n])
                cols_hi[pl.ds(start, tile), n * tile : (n + 1) * tile] = hi
                cols_lo[pl.ds(start, tile), n * tile : (n + 1) * tile] = lo
            return carry

        lax.fori_loop(0, tile_cols - col0, body, 0)

    global_row = a * n_row + row_index
    below = global_row >= LEAD

    def finish(b, value):
        out[:, b * tile : (b + 1) * tile] = value

    @pl.when(below)
    def _():
        start = pl.multiple_of((a - row0) * tile, tile)
        solved = solve_rows(by_row, start, high, low, tile)
        for n in range(LEAD):
            rows_f[n] = solved[n]
        rows = split(jnp.concatenate(solved, axis=1))
        for b in range(tile_cols):
            global_col = b * n_col + col_index
            if b * n_col < LEAD:

                @pl.when(global_col < LEAD)
                def _():
                    finish(b, rows_f[jnp.minimum(global_col, LEAD - 1)])

            if b * n_col + n_col > LEAD:

                @pl.when((global_col >= LEAD) & (global_col <= global_row))
                def _():
                    at = slice((b - col0) * tile, (b - col0 + 1) * tile)
                    update = mm3_nt(rows, (cols_hi[at, :], cols_lo[at, :]))
                    finish(b, work[:, b * tile : (b + 1) * tile] - update)

                @pl.when((global_col >= LEAD) & (global_col > global_row))
                def _():
                    finish(b, jnp.zeros((tile, tile), F32))

    @pl.when(jnp.logical_not(below))
    def _():
        for b in range(tile_cols):
            finish(b, jnp.zeros((tile, tile), F32))

        @pl.when((col_index < LEAD) & (col_index <= row_index))
        def _():
            finish(0, own[...])


def trailing(work, by_row, by_col, high, low, own, spot, tile, n_row, n_col, tile_rows, tile_cols, row0, col0):
    rows, cols = work.shape
    width = LEAD * tile
    count = (tile_cols - col0) * tile
    return pl.pallas_call(
        functools.partial(trailing_kernel, tile, n_row, n_col, tile_cols, row0, col0),
        out_shape=jax.ShapeDtypeStruct((rows, cols), F32),
        grid=(tile_rows,),
        in_specs=[whole(pltpu.SMEM), pl.BlockSpec((tile, cols), lambda a: (a, 0))] + [whole()] * 5,
        out_specs=pl.BlockSpec((tile, cols), lambda a: (a, 0)),
        scratch_shapes=[
            pltpu.VMEM((count, width), BF16),
            pltpu.VMEM((count, width), BF16),
            pltpu.VMEM((LEAD, tile, tile), F32),
        ],
        compiler_params=pltpu.CompilerParams(vmem_limit_bytes=56 << 20),
        cost_estimate=estimate(25, rows * cols * 8),
        name="trailing",
    )(spot, work, by_row, by_col, high, low, own)


def per_device(front_matrix, contributions, target_front, target_row, target_col, live_count):
    tile_rows = front_matrix.shape[1]
    tile = front_matrix.shape[3]
    tile_cols = front_matrix.shape[4]
    n_front = lax.axis_size("front")
    n_row = lax.axis_size("row")
    n_col = lax.axis_size("col")
    spot = jnp.stack([lax.axis_index("row"), lax.axis_index("col")]).astype(jnp.int32)
    front = front_matrix.reshape(tile_rows * tile, tile_cols * tile)
    row0, col0 = LEAD // n_row, LEAD // n_col

    lead = lax.all_gather(front[:tile, :tile], ("row", "col"))
    lead = lead.reshape(n_row, n_col, tile, tile)[:LEAD, :LEAD]
    received, arrived = route_tiles(
        contributions, target_front, target_row, target_col, live_count, tile_cols, n_front, n_row, n_col
    )
    high, low, own = lead_factor(lead, spot, tile, n_row, n_col)
    work = extend(front, received, arrived, tile_rows, tile_cols, tile)
    piece = work[row0 * tile :, :tile]
    by_row = lax.all_gather(piece, "col")[:LEAD]
    mirrored = lax.ppermute(
        piece,
        ("row", "col"),
        [(r * n_col + c, c * n_col + r) for r in range(n_row) for c in range(n_col)],
    )
    by_col = lax.all_gather(mirrored, "row")[:LEAD]
    factor = trailing(
        work, by_row, by_col, high, low, own, spot, tile, n_row, n_col, tile_rows, tile_cols, row0, col0
    )
    return factor.reshape(1, tile_rows, 1, tile, tile_cols, 1, tile)


def solution(mesh):
    in_specs = (
        P("front", None, "row", None, None, "col", None),
        P("front", "row", "col", None, None, None),
        P("front", "row", "col", None),
        P("front", "row", "col", None),
        P("front", "row", "col", None),
        P("front", "row", "col"),
    )
    out_specs = P("front", None, "row", None, None, "col", None)
    return jax.shard_map(
        per_device, mesh=mesh, in_specs=in_specs, out_specs=out_specs, check_vma=False
    )
```

time: 1070 us -> 556 us (0.52)
  other arithmetic: 320 us -> 1.1 us
  Pallas kernels: 0 us -> 283 us
  waiting for transfers between devices: 460 us -> 178 us
  local copies, waits for them, and re-layouts: 175 us -> 33.9 us
  matrix products: 77.9 us -> 0 us
  blocking collectives: 0 us -> 39 us
    psum x6 -> x0, waiting for transfers between devices: 414 us -> none  [the longest x4 326 us: broadcast(): return lax.psum(jnp.where(mine, array, jnp.zeros_like(array)), axis)]
    pallas_call x0 -> x5, Pallas kernels: none -> 283 us  [the longest x1 129 us: route_tiles(): pl.pallas_call(functools.partial(pack_kernel, count, capacity), out_shape...]
    another operation x40 -> x1, other arithmetic: 244 us -> 0.08 us  [per_device(): jnp.stack([lax.axis_index('row'), lax.axis_index('col')]).astype(jnp.int32)]
    ppermute x0 -> x8, waiting for transfers between devices: none -> 178 us  [the longest x1 158 us: per_device(): lax.ppermute(piece, ('row', 'col'), [(r * n_col + c, c * n_col + r) for r...]
    scatter x4 -> x0, local copies, waits for them, and re-layouts: 84.7 us -> none  [per_device(): work = work.at[:, :, local_col, :].set(stored)]
    all_to_all x2 -> x0, waiting for transfers between devices: 46.3 us -> none  [the longest x1 46.3 us: route_tiles(): lax.all_to_all(packed, ('front', 'row'), split_axis=0, concat_axis=0, til...]
    dot_general x3 -> x0, matrix products: 46.2 us -> none  [the longest x2 36.9 us: per_device(): jnp.einsum('atk,bsk->atbs', factor_rows, cols_panel[indices], precision=l...]
    scatter-add x2 -> x0, other arithmetic: 39.2 us -> none  [per_device(): work = work.at[:, :, indices, :].add(-jnp.where(trailing_mask, update, 0.0))]
  transfers between devices with their start and end apart: 8 -> 11, of which waited for: 6 -> 3; matrix products, arithmetic and copies ran while one was open for 10% -> 1% of each run, Pallas kernels for 0% -> 46%
where the time goes in v1:
time: 556 us; the launch traced here: 555 us
  Pallas kernels  283 us (51%)
  waiting for transfers between devices  178 us (32%)
  blocking collectives  39 us (7%)
  local copies, waits for them, and re-layouts  33.9 us (6%)
  between operations  14 us (3%)
  starting transfers between devices  6.13 us (1%)
    ppermute x1, waiting for transfers between devices, per_device(): lax.ppermute(piece, ('row', 'col'), [(r * n_col + c, c * n_col + r) for r...  158 us
    pallas_call x1, Pallas kernels, route_tiles(): pl.pallas_call(functools.partial(pack_kernel, count, capacity), out_shape...  129 us
    pallas_call x1, Pallas kernels, lead_factor(): pl.pallas_call(functools.partial(second_kernel, tile, n_row, n_col), out_...  63.1 us
    pallas_call x1, Pallas kernels, lead_factor(): pl.pallas_call(functools.partial(first_kernel, tile), out_shape=(square,...  52.4 us
    all_gather x1, blocking collectives, route_tiles(): everyone = lax.all_gather(targets.reshape(count, capacity), axes)  39 us
    pallas_call x1, Pallas kernels, trailing(): pl.pallas_call(functools.partial(trailing_kernel, tile, n_row, n_col, til...  29.4 us
    ppermute x7, waiting for transfers between devices, route_tiles(): lax.ppermute(buckets[k], axes, [(i, i ^ k) for i in range(count)])  19.8 us
    unnamed x22, local copies, waits for them, and re-layouts  15.4 us
  transfers between devices with their start and end apart: 11, of which 3 were waited for; matrix products, arithmetic and copies ran while one was open for 1% of the time, Pallas kernels for 46%

profile of v1, /device:TPU:2, one launch (start us, length us, event | category | flops | bytes accessed | tf_op | source)
XLA Modules:
  0.0 555.3 jit_solution(15485466793480702078)
XLA Ops:
  6.5 5.4 copy.18
  12.0 2.0 copy.20
  14.0 2.1 copy-done.5
  16.1 0.7 slice.9
  17.8 0.7 select_reduce_fusion
  18.5 129.1 %pack.1 = (bf16[4,256,256]{2,1,0:T(8,128)(2,1)}, bf16[4,256,256]{2,1,0:T(8,128)(2,1)}, bf16[4,256,256]{2,1,0:T(8,128)(2,1)}, bf16[4,256,256]{2,1,0:T(8,128)(2,1)...) custom-call(s32[32]{0:T(128)} %get-tuple-element.39.source, ...), custom_call_target="tpu_custom_call" | custom-call | tf_op jit(solution)/shard_map/pack/pallas_call | solution.py:221
  147.7 2.0 collective-permute-start.1
  149.7 1.4 collective-permute-start.2
  151.4 11.3 %collective-permute-done.rest_1_ = bf16[4,256,256]{2,1,0:T(8,128)(2,1)S(1)} collective-permute-done((bf16[4,256,256]{2,1,0:T(8,128)(2,1)}, bf16[4,256,256]{2,1,0:T(8,128)(2,1)S(1)}, u32[]{:S(2)}, u32[]{:S(2)}) %collective-permute-start) | collective-permute-done | bytes 524320 | tf_op jit(solution)/shard_map/ppermute | solution.py:232
  162.7 8.5 %collective-permute-done.1.rest_2_ = bf16[4,256,256]{2,1,0:T(8,128)(2,1)S(1)} collective-permute-done((bf16[4,256,256]{2,1,0:T(8,128)(2,1)}, bf16[4,256,256]{2,1,0:T(8,128)(2,1)S(1)}, u32[]{:S(2)}, u32[]{:S(2)}) %collective-permute-start.1) | collective-permute-done | bytes 524320 | tf_op jit(solution)/shard_map/ppermute | solution.py:232
  171.4 39.0 %all_gather.21 = s32[8,8,4]{1,2,0:T(4,128)S(1)} all-gather(s32[1,8,4]{1,2,0:T(4,128)S(1)} %copy.17), channel_id=1, replica_groups=mesh['front'=2,'row'=4,'col'=4] {'front','row'}, dimensions={0}, use_global_device_ids=true | all-gather | bytes 1152 | tf_op jit(solution)/shard_map/all_gather | solution.py:233
  210.9 1.0 copy-done.1
  212.0 9.3 %extend.1.work = f32[1536,1536]{1,0:T(8,128)} custom-call(s32[32]{0:T(128)S(1)} %reshape.181.arrived, bf16[1536,1536]{1,0:T(8,128)(2,1)} %bitcast.55, bf16[4,256,256]{2,1,0:T(8,128)(2,1)S(1)} %copy-done.1, bf16[4,256,256]{2,1,0:T(8,128)(2,1)S(1)} %collective-permute-done.rest_1_, bf16[4,256,256]{2,1,0:T(8,128)(2,1)S(1)} %collective-permute-done.1.rest_2_, ...), custom_call_target="tpu_custom_call" | custom-call | flops 8000000000 | bytes 14155776 | tf_op jit(solution)/shard_map/extend/pallas_call | solution.py:258
  221.3 2.5 slice.8
  223.8 2.3 collective-permute-start.7
  226.2 157.9 %collective-permute-done.7 = f32[1280,256]{1,0:T(8,128)S(1)} collective-permute-done((f32[1280,256]{1,0:T(8,128)}, f32[1280,256]{1,0:T(8,128)S(1)}, u32[]{:S(2)}, u32[]{:S(2)}) %collective-permute-start.7) | collective-permute-done | bytes 1310752 | tf_op jit(solution)/shard_map/ppermute | solution.py:387
  384.1 1.1 copy-done.6
  385.3 1.6 copy-done
  386.9 52.4 %lead_first.1 = (f32[512,512]{1,0:T(8,128)S(1)}, f32[512,512]{1,0:T(8,128)S(1)}) custom-call(bf16[4,4,256,256]{3,2,1,0:T(8,128)(2,1)S(1)} %bitcast.52), custom_call_target="tpu_custom_call" | custom-call | flops 60000002048 | bytes 1048576 | tf_op jit(solution)/shard_map/lead_first/pallas_call | solution.py:153
  439.4 63.1 %lead_second.1 = (bf16[1024,1024]{1,0:T(8,128)(2,1)S(1)}, bf16[1024,1024]{1,0:T(8,128)(2,1)}, f32[256,256]{1,0:T(8,128)S(1)}) custom-call(s32[2]{0:T(128)S(1)} %pad_add_fusion.spot, bf16[4,4,256,256]{3,2,1,0:T(8,128)(2,1)} %bitcast.51, f32[512,512]{1,0:T(8,128)S(1)} %get-tuple-element.26.lower0, f32[512,512]{1,0:T(8,128)S(1)} %get-tuple-element.27.inverse0), custom_call_target="tpu_custom_call" | custom-call | flops 60000002048 | bytes 1048576 | tf_op jit(solution)/shard_map/lead_second/pallas_call | solution.py:164
  502.4 1.4 copy-done.3
  503.8 0.7 copy-done.4
  504.5 29.4 %trailing.1 = f32[1536,1536]{1,0:T(8,128)} custom-call(s32[2]{0:T(128)} %copy-done.2, f32[1536,1536]{1,0:T(8,128)} %extend.1.work, f32[4,1280,256]{2,1,0:T(8,128)} %bitcast.65, f32[4,1280,256]{2,1,0:T(8,128)} %bitcast.66, bf16[1024,1024]{1,0:T(8,128)(2,1)} %copy-done.3, bf16[1024,1024]{1,0:T(8,128)(2,1)} %get-tuple-element.29.low, f32[256,256]{1,0:T(8,128)} %copy-done.4), custom_call_target="tpu_custom_call" | custom-call | flops 24999999488 | bytes 18874368 | tf_op jit(solution)/shard_map/trailing/pallas_call | solution.py:350
  533.9 14.9 %reshape.190 = f32[1,6,1,256,6,1,256]{6,5,4,3,2,1,0:T(1,128)} reshape(f32[1536,1536]{1,0:T(8,128)} %trailing.1) | data formatting | bytes 18874368 | tf_op jit(solution)/shard_map/reshape | solution.py:396
  (45 shorter events, 1.4 us)
Async XLA Ops:
  6.5 378.8 %all-gather.11.cloned.1.call-start = ((), (), s32[]{:S(2)}) async-start(), calls=%async_computation.2 | async-start | bytes 2228224 | tf_op jit(solution)/shard_map/all_gather | solution.py:378
  11.9 5.6 %copy-start.7 = (s32[1,1,1,32]{3,2,1,0:T(1,128)S(1)}, s32[1,1,1,32]{3,2,1,0:T(1,128)}, u32[]{:S(2)}) copy-start(s32[1,1,1,32]{3,2,1,0:T(1,128)} %param.10) | copy-start | bytes 388
  11.9 5.6 %copy-start.8 = (s32[1,1,1,32]{3,2,1,0:T(1,128)S(1)}, s32[1,1,1,32]{3,2,1,0:T(1,128)}, u32[]{:S(2)}) copy-start(s32[1,1,1,32]{3,2,1,0:T(1,128)} %param.9) | copy-start | bytes 388
  12.0 5.6 %copy-start.9 = (s32[1,1,1,32]{3,2,1,0:T(1,128)S(1)}, s32[1,1,1,32]{3,2,1,0:T(1,128)}, u32[]{:S(2)}) copy-start(s32[1,1,1,32]{3,2,1,0:T(1,128)} %param.8) | copy-start | bytes 388
  14.0 2.1 copy-start.5
  16.8 487.7 %all-gather.7.cloned.1.call-start = ((), (), s32[]{:S(2)}) async-start(), calls=%async_computation | async-start | bytes 6553600 | tf_op jit(solution)/shard_map/all_gather | solution.py:386
  147.6 15.1 %collective-permute-start = (bf16[4,256,256]{2,1,0:T(8,128)(2,1)}, bf16[4,256,256]{2,1,0:T(8,128)(2,1)S(1)}, u32[]{:S(2)}, u32[]{:S(2)}) collective-permute-start(bf16[4,256,256]{2,1,0:T(8,128)(2,1)} %get-tuple-element.19), channel_id=1, source_target_pairs={{0,4},{4,0},{8,12},{12,8},{16,20},{20,16},{24,28},{28,24},{1,5},{5... | collective-permute-start | bytes 1572872 | tf_op jit(solution)/shard_map/ppermute | solution.py:232
  147.7 23.5 %collective-permute-start.1 = (bf16[4,256,256]{2,1,0:T(8,128)(2,1)}, bf16[4,256,256]{2,1,0:T(8,128)(2,1)S(1)}, u32[]{:S(2)}, u32[]{:S(2)}) collective-permute-start(bf16[4,256,256]{2,1,0:T(8,128)(2,1)} %get-tuple-element.20), channel_id=1, source_target_pairs={{0,8},{4,12},{8,0},{12,4},{16,24},{20,28},{24,16},{28,20},{1,9},{5... | collective-permute-start | bytes 1572872 | tf_op jit(solution)/shard_map/ppermute | solution.py:232
  149.7 61.1 %collective-permute-start.2 = (bf16[4,256,256]{2,1,0:T(8,128)(2,1)}, bf16[4,256,256]{2,1,0:T(8,128)(2,1)S(1)}, u32[]{:S(2)}, u32[]{:S(2)}) collective-permute-start(bf16[4,256,256]{2,1,0:T(8,128)(2,1)} %get-tuple-element.21), channel_id=1, source_target_pairs={{0,12},{4,8},{8,4},{12,0},{16,28},{20,24},{24,20},{28,16},{1,13},{... | collective-permute-start | bytes 1572872 | tf_op jit(solution)/shard_map/ppermute | solution.py:232
  151.2 59.7 %collective-permute-start.3 = (bf16[4,256,256]{2,1,0:T(8,128)(2,1)}, bf16[4,256,256]{2,1,0:T(8,128)(2,1)S(1)}, u32[]{:S(2)}, u32[]{:S(2)}) collective-permute-start(bf16[4,256,256]{2,1,0:T(8,128)(2,1)} %get-tuple-element.22), channel_id=1, source_target_pairs={{0,16},{4,20},{8,24},{12,28},{16,0},{20,4},{24,8},{28,12},{1,17},{... | collective-permute-start | bytes 1572872 | tf_op jit(solution)/shard_map/ppermute | solution.py:232
  151.2 59.7 %collective-permute-start.4 = (bf16[4,256,256]{2,1,0:T(8,128)(2,1)}, bf16[4,256,256]{2,1,0:T(8,128)(2,1)S(1)}, u32[]{:S(2)}, u32[]{:S(2)}) collective-permute-start(bf16[4,256,256]{2,1,0:T(8,128)(2,1)} %get-tuple-element.23), channel_id=1, source_target_pairs={{0,20},{4,16},{8,28},{12,24},{16,4},{20,0},{24,12},{28,8},{1,21},{... | collective-permute-start | bytes 1572872 | tf_op jit(solution)/shard_map/ppermute | solution.py:232
  162.7 48.2 %collective-permute-start.5 = (bf16[4,256,256]{2,1,0:T(8,128)(2,1)}, bf16[4,256,256]{2,1,0:T(8,128)(2,1)S(1)}, u32[]{:S(2)}, u32[]{:S(2)}) collective-permute-start(bf16[4,256,256]{2,1,0:T(8,128)(2,1)} %get-tuple-element.24), channel_id=1, source_target_pairs={{0,24},{4,28},{8,16},{12,20},{16,8},{20,12},{24,0},{28,4},{1,25},{... | collective-permute-start | bytes 1572872 | tf_op jit(solution)/shard_map/ppermute | solution.py:232
  171.1 39.8 %collective-permute-start.6 = (bf16[4,256,256]{2,1,0:T(8,128)(2,1)}, bf16[4,256,256]{2,1,0:T(8,128)(2,1)}, u32[]{:S(2)}, u32[]{:S(2)}) collective-permute-start(bf16[4,256,256]{2,1,0:T(8,128)(2,1)} %get-tuple-element.25), channel_id=1, source_target_pairs={{0,28},{4,24},{8,20},{12,16},{16,12},{20,8},{24,4},{28,0},{1,29},{... | collective-permute-start | bytes 1572872 | tf_op jit(solution)/shard_map/ppermute | solution.py:232
  210.9 1.0 copy-start.1
  223.7 280.8 %all-gather.9.cloned.1.call-start = ((), (), s32[]{:S(2)}) async-start(), calls=%async_computation.1 | async-start | bytes 6553600 | tf_op jit(solution)/shard_map/all_gather | solution.py:392
  223.8 160.3 %collective-permute-start.7 = (f32[1280,256]{1,0:T(8,128)}, f32[1280,256]{1,0:T(8,128)S(1)}, u32[]{:S(2)}, u32[]{:S(2)}) collective-permute-start(f32[1280,256]{1,0:T(8,128)} %slice.8), channel_id=1, source_target_pairs={{0,0},{1,4},{2,8},{3,12},{4,1},{5,5},{6,9},{7,13},{8,2},{9,6},{10,... | collective-permute-start | bytes 3932168 | tf_op jit(solution)/shard_map/ppermute | solution.py:387
  226.2 213.2 %copy-start.2 = (s32[2]{0:T(128)}, s32[2]{0:T(128)S(1)}, u32[]{:S(2)}) copy-start(s32[2]{0:T(128)S(1)} %pad_add_fusion.spot) | copy-start | bytes 28
  384.1 1.2 copy-start.6
  385.3 1.6 copy-start
  502.4 1.4 copy-start.3
  503.8 0.7 copy-start.4
Sparse Core Ops, SparseCore 0:
  16.9 61.7 all-gather.10
  223.9 146.6 all-gather.6
  385.4 75.6 all-gather.8

commit v2 on v1

--- a/solution.py
+++ b/solution.py
@@ -11,6 +11,8 @@
 PANELS = 2
 LEAD = PANEL_TILES * PANELS
 BLOCK = 128
+LANES = 128
+TOP = 32000.0
 HIGHEST = lax.Precision.HIGHEST
 NT = (((1,), (1,)), ((), ()))
 F32 = jnp.float32
@@ -99,24 +101,30 @@
     lax.fori_loop(0, size // BLOCK, step, 0)
 
 
-def load_square(lead, work, row0, col0, tile):
-    for i in range(PANEL_TILES):
-        for j in range(PANEL_TILES):
-            work[i * tile : (i + 1) * tile, j * tile : (j + 1) * tile] = lead[
-                row0 + i, col0 + j
-            ].astype(F32)
-
-
-def first_kernel(tile, lead, lower, inverse, work):
-    load_square(lead, work, 0, 0, tile)
+def load_square(spot, lead, work, row0, col0, tile):
+    for k, tiles in enumerate(lead):
+        row = jnp.bitwise_xor(spot[0], k) - row0
+
+        @pl.when((row >= 0) & (row < PANEL_TILES))
+        def _():
+            at = pl.ds(pl.multiple_of(row * tile, tile), tile)
+            for j in range(PANEL_TILES):
+                place = jnp.bitwise_xor(spot[1], col0 + j)
+                work[at, j * tile : (j + 1) * tile] = tiles[place].astype(F32)
+
+
+def first_kernel(tile, n_row, spot, *rest):
+    lead, (lower, inverse, work) = rest[:n_row], rest[n_row:]
+    load_square(spot, lead, work, 0, 0, tile)
     factor_panel(work, lower, inverse, 0)
 
 
-def second_kernel(tile, n_row, n_col, spot, lead, lower0, inverse0, high, low, own, work, lower, inverse):
+def second_kernel(tile, n_row, spot, *rest):
+    lead, (lower0, inverse0, high, low, own, work, lower, inverse) = rest[:n_row], rest[n_row:]
     width = PANEL_TILES * tile
-    load_square(lead, work, PANEL_TILES, 0, tile)
+    load_square(spot, lead, work, PANEL_TILES, 0, tile)
     left = mm_nt(work[...], inverse0[...])
-    load_square(lead, work, PANEL_TILES, PANEL_TILES, tile)
+    load_square(spot, lead, work, PANEL_TILES, PANEL_TILES, tile)
     work[...] -= mm_nt(left, left)
     lower[:width, :width] = lower0[...]
     lower[:width, width:] = jnp.zeros((width, width), F32)
@@ -146,55 +154,58 @@
     return pl.CostEstimate(flops=int(us * 1e9), bytes_accessed=size, transcendentals=0)
 
 
-def lead_factor(lead, spot, tile, n_row, n_col):
+def lead_first(lead, spot, tile):
     width = PANEL_TILES * tile
     square = jax.ShapeDtypeStruct((width, width), F32)
-    params = pltpu.CompilerParams(vmem_limit_bytes=48 << 20)
-    lower0, inverse0 = pl.pallas_call(
-        functools.partial(first_kernel, tile),
+    return pl.pallas_call(
+        functools.partial(first_kernel, tile, len(lead)),
         out_shape=(square, square),
-        in_specs=[whole()],
+        in_specs=[whole(pltpu.SMEM)] + [whole()] * len(lead),
         out_specs=(whole(), whole()),
         scratch_shapes=[pltpu.VMEM((width, width), F32)],
-        compiler_params=params,
+        compiler_params=pltpu.CompilerParams(vmem_limit_bytes=48 << 20),
         cost_estimate=estimate(60, 1 << 20),
         name="lead_first",
-    )(lead)
+    )(spot, *lead)
+
+
+def lead_second(lead, lower0, inverse0, spot, tile):
+    width = PANEL_TILES * tile
     full = (2 * width, 2 * width)
-    high, low, own = pl.pallas_call(
-        functools.partial(second_kernel, tile, n_row, n_col),
+    return pl.pallas_call(
+        functools.partial(second_kernel, tile, len(lead)),
         out_shape=(
             jax.ShapeDtypeStruct(full, BF16),
             jax.ShapeDtypeStruct(full, BF16),
             jax.ShapeDtypeStruct((tile, tile), F32),
         ),
-        in_specs=[whole(pltpu.SMEM)] + [whole()] * 3,
+        in_specs=[whole(pltpu.SMEM)] + [whole()] * (len(lead) + 2),
         out_specs=(whole(),) * 3,
         scratch_shapes=[
             pltpu.VMEM((width, width), F32),
             pltpu.VMEM(full, F32),
             pltpu.VMEM((width, width), F32),
         ],
-        compiler_params=params,
+        compiler_params=pltpu.CompilerParams(vmem_limit_bytes=48 << 20),
         cost_estimate=estimate(60, 1 << 20),
         name="lead_second",
-    )(spot, lead, lower0, inverse0)
-    return high, low, own
+    )(spot, *lead, lower0, inverse0)
 
 
 def pack_kernel(count, capacity, source, tiles, *rest):
-    buckets, sems = rest[:count], rest[count]
-    copies = []
-    for k in range(count):
-        for p in range(capacity):
-            n = k * capacity + p
-            copies.append(
-                pltpu.make_async_copy(tiles.at[source[n]], buckets[k].at[p], sems.at[n])
-            )
-    for copy in copies:
-        copy.start()
-    for copy in copies:
-        copy.wait()
+    buckets, (held, in_sems, out_sems) = rest[:count], rest[count:]
+    loads, stores = [], []
+    for n in range(count * capacity):
+        loads.append(pltpu.make_async_copy(tiles.at[source[n]], held.at[n], in_sems.at[n]))
+        into = buckets[n // capacity].at[n % capacity]
+        stores.append(pltpu.make_async_copy(held.at[n], into, out_sems.at[n]))
+    for load in loads:
+        load.start()
+    for load, store in zip(loads, stores):
+        load.wait()
+        store.start()
+    for store in stores:
+        store.wait()
 
 
 def route_tiles(contributions, target_front, target_row, target_col, live_count, tile_cols, n_front, n_row, n_col):
@@ -223,7 +234,13 @@
         out_shape=tuple(jax.ShapeDtypeStruct((capacity, tile, tile), BF16) for _ in range(count)),
         in_specs=[whole(pltpu.SMEM), whole(pl.ANY)],
         out_specs=tuple(whole(pl.ANY) for _ in range(count)),
-        scratch_shapes=[pltpu.SemaphoreType.DMA((count * capacity,))],
+        scratch_shapes=[
+            pltpu.VMEM((count * capacity, tile, tile), BF16),
+            pltpu.SemaphoreType.DMA((count * capacity,)),
+            pltpu.SemaphoreType.DMA((count * capacity,)),
+        ],
+        compiler_params=pltpu.CompilerParams(vmem_limit_bytes=16 << 20),
+        cost_estimate=estimate(5, 2 * slots * tile * tile * 2),
         name="pack",
     )(source, tiles)
     axes = ("front", "row")
@@ -267,8 +284,13 @@
     )(arrived, front, *received)
 
 
-def solve_rows(gathered, start, high, low, tile):
-    parts = [split(gathered[c, pl.ds(start, tile), :]) for c in range(LEAD)]
+def solve_rows(coded, scales, index, t, high, low, tile):
+    start = pl.multiple_of(t * tile, tile)
+    parts = []
+    for c in range(LEAD):
+        k = jnp.bitwise_xor(index, c)
+        values = coded[k, pl.ds(start, tile), :].astype(jnp.int32).astype(F32)
+        parts.append(split(values * scales[k, t]))
     solved = []
     for n in range(LEAD):
         total = None
@@ -282,16 +304,17 @@
 
 
 def trailing_kernel(
-    tile, n_row, n_col, tile_cols, row0, col0, spot, work, by_row, by_col, high, low, own, out, cols_hi, cols_lo, rows_f
+    tile, n_row, n_col, tile_cols, row0, col0, spot, row_scales, col_scales, work, by_row, by_col, high, low, own, out, cols_hi, cols_lo, rows_f
 ):
     a = pl.program_id(0)
     row_index, col_index = spot[0], spot[1]
+    pieces = tile // LANES
 
     @pl.when(a == 0)
     def _():
         def body(b, carry):
             start = pl.multiple_of(b * tile, tile)
-            solved = solve_rows(by_col, start, high, low, tile)
+            solved = solve_rows(by_col, col_scales, row_index, b, high, low, tile)
             for n in range(LEAD):
                 hi, lo = split(solved[n])
                 cols_hi[pl.ds(start, tile), n * tile : (n + 1) * tile] = hi
@@ -304,12 +327,13 @@
     below = global_row >= LEAD
 
     def finish(b, value):
-        out[:, b * tile : (b + 1) * tile] = value
+        for part in range(pieces):
+            lanes = value[:, part * LANES : (part + 1) * LANES]
+            out[pl.ds(b * pieces + part, tile, stride=tile_cols * pieces), :] = lanes
 
     @pl.when(below)
     def _():
-        start = pl.multiple_of((a - row0) * tile, tile)
-        solved = solve_rows(by_row, start, high, low, tile)
+        solved = solve_rows(by_row, row_scales, col_index, a - row0, high, low, tile)
         for n in range(LEAD):
             rows_f[n] = solved[n]
         rows = split(jnp.concatenate(solved, axis=1))
@@ -347,12 +371,15 @@
     rows, cols = work.shape
     width = LEAD * tile
     count = (tile_cols - col0) * tile
+    lines = tile * cols // LANES
     return pl.pallas_call(
         functools.partial(trailing_kernel, tile, n_row, n_col, tile_cols, row0, col0),
-        out_shape=jax.ShapeDtypeStruct((rows, cols), F32),
+        out_shape=jax.ShapeDtypeStruct((tile_rows * lines, LANES), F32),
         grid=(tile_rows,),
-        in_specs=[whole(pltpu.SMEM), pl.BlockSpec((tile, cols), lambda a: (a, 0))] + [whole()] * 5,
-        out_specs=pl.BlockSpec((tile, cols), lambda a: (a, 0)),
+        in_specs=[whole(pltpu.SMEM)] * 3
+        + [pl.BlockSpec((tile, cols), lambda a: (a, 0))]
+        + [whole()] * 5,
+        out_specs=pl.BlockSpec((lines, LANES), lambda a: (a, 0)),
         scratch_shapes=[
             pltpu.VMEM((count, width), BF16),
             pltpu.VMEM((count, width), BF16),
@@ -361,7 +388,29 @@
         compiler_params=pltpu.CompilerParams(vmem_limit_bytes=56 << 20),
         cost_estimate=estimate(25, rows * cols * 8),
         name="trailing",
-    )(spot, work, by_row, by_col, high, low, own)
+    )(spot, decode_scales(by_row, tile), decode_scales(by_col, tile), work, by_row, by_col, high, low, own)
+
+
+def encode(piece, tile):
+    tiles = piece.reshape(-1, tile, tile)
+    largest = jnp.max(jnp.abs(tiles), axis=(1, 2))
+    power = jnp.floor(jnp.log2(jnp.maximum(largest, 1e-30))) + 1.0
+    half = jnp.floor(0.5 * power)
+    shrunk = tiles * jnp.exp2(-half)[:, None, None]
+    codes = jnp.round(shrunk * (jnp.exp2(half - power) * TOP)[:, None, None]).astype(jnp.int16)
+    line = jnp.zeros((16, tile), jnp.int16).at[0, : tiles.shape[0]].set(power.astype(jnp.int16))
+    return jnp.concatenate([codes.reshape(-1, tile), line], axis=0)
+
+
+def decode_scales(coded, tile):
+    rows = coded.shape[1] - 16
+    return jnp.exp2(coded[:, rows, : rows // tile].astype(F32) - 14.0) * (16384.0 / TOP)
+
+
+def exchange(piece, axis, size):
+    return [piece] + [
+        lax.ppermute(piece, axis, [(i, i ^ k) for i in range(size)]) for k in range(1, size)
+    ]
 
 
 def per_device(front_matrix, contributions, target_front, target_row, target_col, live_count):
@@ -372,26 +421,41 @@
     n_row = lax.axis_size("row")
     n_col = lax.axis_size("col")
     spot = jnp.stack([lax.axis_index("row"), lax.axis_index("col")]).astype(jnp.int32)
+    row0, col0 = LEAD // n_row, LEAD // n_col
+
+    line = jnp.stack(exchange(front_matrix[0, 0, 0, :, 0, 0, :], "col", n_col))
+    lead = exchange(line, "row", n_row)
     front = front_matrix.reshape(tile_rows * tile, tile_cols * tile)
-    row0, col0 = LEAD // n_row, LEAD // n_col
-
-    lead = lax.all_gather(front[:tile, :tile], ("row", "col"))
-    lead = lead.reshape(n_row, n_col, tile, tile)[:LEAD, :LEAD]
     received, arrived = route_tiles(
         contributions, target_front, target_row, target_col, live_count, tile_cols, n_front, n_row, n_col
     )
-    high, low, own = lead_factor(lead, spot, tile, n_row, n_col)
+    lower0, inverse0 = lead_first(lead, spot, tile)
+    arrived, lower0 = lax.optimization_barrier((arrived, lower0))
     work = extend(front, received, arrived, tile_rows, tile_cols, tile)
-    piece = work[row0 * tile :, :tile]
-    by_row = lax.all_gather(piece, "col")[:LEAD]
+    coded = encode(work[row0 * tile :, :tile], tile)
+    by_row = exchange(coded, "col", n_col)
     mirrored = lax.ppermute(
-        piece,
+        coded,
         ("row", "col"),
         [(r * n_col + c, c * n_col + r) for r in range(n_row) for c in range(n_col)],
     )
-    by_col = lax.all_gather(mirrored, "row")[:LEAD]
+    by_col = exchange(mirrored, "row", n_row)
+    high, low, own = lead_second(lead, lower0, inverse0, spot, tile)
     factor = trailing(
-        work, by_row, by_col, high, low, own, spot, tile, n_row, n_col, tile_rows, tile_cols, row0, col0
+        work,
+        jnp.stack(by_row),
+        jnp.stack(by_col),
+        high,
+        low,
+        own,
+        spot,
+        tile,
+        n_row,
+        n_col,
+        tile_rows,
+        tile_cols,
+        row0,
+        col0,
     )
     return factor.reshape(1, tile_rows, 1, tile, tile_cols, 1, tile)
 

time: 556 us -> 328 us (0.59)
  the two profiles are of different devices: /device:TPU:2 before, /device:TPU:20 now
where the time goes in v2:
time: 328 us; the launch traced here: 327 us
  Pallas kernels  166 us (51%)
  starting transfers between devices  81.9 us (25%)
  blocking collectives  35.7 us (11%)
  local copies, waits for them, and re-layouts  23.6 us (7%)
  waiting for transfers between devices  11.9 us (4%)
  other arithmetic  7.56 us (2%)
    ppermute x12, starting transfers between devices, exchange(): lax.ppermute(piece, axis, [(i, i ^ k) for i in range(size)])  74.5 us
    pallas_call x1, Pallas kernels, lead_second(): pl.pallas_call(functools.partial(second_kernel, tile, len(lead)), out_sha...  63 us
    pallas_call x1, Pallas kernels, lead_first(): pl.pallas_call(functools.partial(first_kernel, tile, len(lead)), out_shap...  53.2 us
    all_gather x1, blocking collectives, route_tiles(): everyone = lax.all_gather(targets.reshape(count, capacity), axes)  35.7 us
    pallas_call x1, Pallas kernels, trailing(): pl.pallas_call(functools.partial(trailing_kernel, tile, n_row, n_col, til...  28 us
    unnamed x40, local copies, waits for them, and re-layouts  22 us
    ppermute x12, waiting for transfers between devices, exchange(): lax.ppermute(piece, axis, [(i, i ^ k) for i in range(size)])  11.9 us
    pallas_call x1, Pallas kernels, route_tiles(): pl.pallas_call(functools.partial(pack_kernel, count, capacity), out_shape...  11.6 us
  transfers between devices with their start and end apart: 20, of which 1 were waited for; matrix products, arithmetic and copies ran while one was open for 6% of the time, Pallas kernels for 39%

profile of v2, /device:TPU:20, one launch (start us, length us, event | category | flops | bytes accessed | tf_op | source)
XLA Modules:
  0.0 327.2 jit_solution(7549986067401211355)
XLA Ops:
  1.4 3.5 %collective-permute-start.1 = (bf16[256,256]{1,0:T(8,128)(2,1)S(1)}, bf16[256,256]{1,0:T(8,128)(2,1)}, u32[]{:S(2)}, u32[]{:S(2)}) collective-permute-start(bf16[256,256]{1,0:T(8,128)(2,1)S(1)} %get-tuple-element.60), channel_id=1, source_target_pairs={{0,2},{1,3},{2,0},{3,1},{4,6},{5,7},{6,4},{7,5},{8,10},{9,11},{10,... | collective-permute-start | bytes 393224 | tf_op jit(solution)/shard_map/ppermute | solution.py:412
  6.6 2.2 copy-done
  8.8 11.6 %pack.1 = (bf16[4,256,256]{2,1,0:T(8,128)(2,1)S(1)}, bf16[4,256,256]{2,1,0:T(8,128)(2,1)}, bf16[4,256,256]{2,1,0:T(8,128)(2,1)}, bf16[4,256,256]{2,1,0:T(8,128)(...) custom-call(s32[32]{0:T(128)S(1)} %get-tuple-element.55.source, ...), custom_call_target="tpu_custom_call" | custom-call | flops 5000000000 | bytes 8388608 | tf_op jit(solution)/shard_map/pack/pallas_call | solution.py:232
  22.8 1.5 collective-permute-start.6
  24.8 1.0 pad_maximum_fusion.rest_0_
  25.9 1.6 collective-permute-start.5
  27.9 1.5 collective-permute-start.3
  29.4 8.1 %copy.18 = bf16[1,6,1,256,6,1,256]{6,4,3,1,5,2,0:T(8,128)(2,1)} copy(bf16[1,6,1,256,6,1,256]{6,3,5,4,2,1,0:T(8,128)(2,1)} %param.8) | data formatting | bytes 9437184 | tf_op args[0]
  37.8 35.7 %all_gather.3 = s32[8,8,4]{1,2,0:T(4,128)S(1)} all-gather(s32[1,8,4]{1,2,0:T(4,128)S(1)} %copy.17), channel_id=1, replica_groups=mesh['front'=2,'row'=4,'col'=4] {'front','row'}, dimensions={0}, use_global_device_ids=true | all-gather | bytes 1152 | tf_op jit(solution)/shard_map/all_gather | solution.py:250
  73.9 7.2 %copy.20 = bf16[192,8,6,256]{3,1,2,0:T(8,128)(2,1)} copy(bf16[192,8,6,256]{3,2,1,0:T(8,128)(2,1)} %bitcast.70) | data formatting | bytes 9437184
  81.2 1.3 collective-permute-start.8
  82.7 1.0 collective-permute-start.10
  84.6 1.3 collective-permute-start.12
  85.9 53.2 %lead_first.1 = (f32[512,512]{1,0:T(8,128)S(1)}, f32[512,512]{1,0:T(8,128)S(1)}) custom-call(s32[2]{0:T(128)S(1)} %pad_add_fusion.3.spot, bf16[4,256,256]{2,1,0:T(8,128)(2,1)S(1)} %pad_maximum_fusion.rest_0_, bf16[4,256,256]{2,1,0:T(8,128)(2,1)S(1)} %collective-permute-done.3.rest_1_, bf16[4,256,256]{2,1,0:T(8,128)(2,1)S(1)} %collective-permute-done.4.rest_2_, ...), custom_call_target="tpu_custom_call" | custom-call | flops 60000002048 | bytes 1048576 | tf_op jit(solution)/shard_map/lead_first/pallas_call | solution.py:160
  139.2 9.9 %extend.1.work = f32[1536,1536]{1,0:T(8,128)} custom-call(s32[32]{0:T(128)S(1)} %reshape.262.arrived, bf16[1536,1536]{1,0:T(8,128)(2,1)} %bitcast.71, bf16[4,256,256]{2,1,0:T(8,128)(2,1)S(1)} %copy-done.11, bf16[4,256,256]{2,1,0:T(8,128)(2,1)S(1)} %collective-permute-done.6.rest_1_, bf16[4,256,256]{2,1,0:T(8,128)(2,1)} %collective-permute-done.7.rest_2_, ...), custom_call_target="tpu_custom_call" | custom-call | flops 8000000000 | bytes 14155776 | tf_op jit(solution)/shard_map/extend/pallas_call | solution.py:275
  149.2 1.6 abs_reduce_fusion
  151.0 1.9 round-nearest-even_convert_fusion
  153.7 4.4 %collective-permute-start.15 = (s16[1296,256]{1,0:T(8,128)(2,1)S(1)}, s16[1296,256]{1,0:T(8,128)(2,1)S(1)}, u32[]{:S(2)}, u32[]{:S(2)}) collective-permute-start(s16[1296,256]{1,0:T(8,128)(2,1)S(1)} %get-tuple-element.62), channel_id=1, source_target_pairs={{0,3},{1,2},{2,1},{3,0},{4,7},{5,6},{6,5},{7,4},{8,11},{9,10},{10,... | collective-permute-start | bytes 1990664 | tf_op jit(solution)/shard_map/ppermute | solution.py:412
  158.1 1.8 collective-permute-start.14
  160.6 58.3 %collective-permute-start.19 = (s16[1296,256]{1,0:T(8,128)(2,1)S(1)}, s16[1296,256]{1,0:T(8,128)(2,1)S(1)}, u32[]{:S(2)}, u32[]{:S(2)}) collective-permute-start(s16[1296,256]{1,0:T(8,128)(2,1)S(1)} %collective-permute-done.16), channel_id=1, source_target_pairs={{0,12},{4,8},{8,4},{12,0},{1,13},{5,9},{9,5},{13,1},{2,14},{6,10},... | collective-permute-start | bytes 1990664 | tf_op jit(solution)/shard_map/ppermute | solution.py:412
  218.9 11.9 %collective-permute-done.15 = s16[1296,256]{1,0:T(8,128)(2,1)S(1)} collective-permute-done((s16[1296,256]{1,0:T(8,128)(2,1)S(1)}, s16[1296,256]{1,0:T(8,128)(2,1)S(1)}, u32[]{:S(2)}, u32[]{:S(2)}) %collective-permute-start.15) | collective-permute-done | bytes 663584 | tf_op jit(solution)/shard_map/ppermute | solution.py:412
  230.7 1.8 collective-permute-start.17
  232.5 63.0 %lead_second.1 = (bf16[1024,1024]{1,0:T(8,128)(2,1)}, bf16[1024,1024]{1,0:T(8,128)(2,1)}, f32[256,256]{1,0:T(8,128)S(1)}) custom-call(s32[2]{0:T(128)S(1)} %pad_add_fusion.3.spot, bf16[4,256,256]{2,1,0:T(8,128)(2,1)S(1)} %pad_maximum_fusion.rest_0_, bf16[4,256,256]{2,1,0:T(8,128)(2,1)S(1)} %collective-permute-done.3.rest_1_, ...), custom_call_target="tpu_custom_call" | custom-call | flops 60000002048 | bytes 1048576 | tf_op jit(solution)/shard_map/lead_second/pallas_call | solution.py:175
  299.2 28.0 %trailing.1 = f32[18432,128]{1,0:T(8,128)} custom-call(s32[2]{0:T(128)} %copy-done.9, f32[4,5]{1,0:T(4,128)} %bitcast.88, f32[4,5]{1,0:T(4,128)} %bitcast.89, f32[1536,1536]{1,0:T(8,128)} %extend.1.work, s16[4,1296,256]{2,1,0:T(8,128)(2,1)} %copy-done.17, s16[4,1296,256]{2,1,0:T(8,128)(2,1)} %copy-done.18, bf16[1024,1024]{1,0:T(8,128)(2,1)} %get-tuple-element.44.high, ...), custom_call_target="tpu_custom_call" | custom-call | flops 24999999488 | bytes 18874368 | tf_op jit(solution)/shard_map/trailing/pallas_call | solution.py:375
  (92 shorter events, 13.1 us)
Async XLA Ops:
  0.9 23.9 %collective-permute-start.2 = (bf16[256,256]{1,0:T(8,128)(2,1)S(1)}, bf16[256,256]{1,0:T(8,128)(2,1)S(1)}, u32[]{:S(2)}, u32[]{:S(2)}) collective-permute-start(bf16[256,256]{1,0:T(8,128)(2,1)S(1)} %get-tuple-element.60), channel_id=1, source_target_pairs={{0,3},{1,2},{2,1},{3,0},{4,7},{5,6},{6,5},{7,4},{8,11},{9,10},{10,... | collective-permute-start | bytes 393224 | tf_op jit(solution)/shard_map/ppermute | solution.py:412
  1.4 23.4 %collective-permute-start.1 = (bf16[256,256]{1,0:T(8,128)(2,1)S(1)}, bf16[256,256]{1,0:T(8,128)(2,1)}, u32[]{:S(2)}, u32[]{:S(2)}) collective-permute-start(bf16[256,256]{1,0:T(8,128)(2,1)S(1)} %get-tuple-element.60), channel_id=1, source_target_pairs={{0,2},{1,3},{2,0},{3,1},{4,6},{5,7},{6,4},{7,5},{8,10},{9,11},{10,... | collective-permute-start | bytes 393224 | tf_op jit(solution)/shard_map/ppermute | solution.py:412
  4.9 19.9 %collective-permute-start = (bf16[256,256]{1,0:T(8,128)(2,1)S(1)}, bf16[256,256]{1,0:T(8,128)(2,1)}, u32[]{:S(2)}, u32[]{:S(2)}) collective-permute-start(bf16[256,256]{1,0:T(8,128)(2,1)S(1)} %get-tuple-element.60), channel_id=1, source_target_pairs={{0,1},{1,0},{2,3},{3,2},{4,5},{5,4},{6,7},{7,6},{8,9},{9,8},{10,11... | collective-permute-start | bytes 393224 | tf_op jit(solution)/shard_map/ppermute | solution.py:412
  22.8 58.4 %collective-permute-start.6 = (bf16[4,256,256]{2,1,0:T(8,128)(2,1)}, bf16[4,256,256]{2,1,0:T(8,128)(2,1)S(1)}, u32[]{:S(2)}, u32[]{:S(2)}) collective-permute-start(bf16[4,256,256]{2,1,0:T(8,128)(2,1)} %get-tuple-element.35), channel_id=1, source_target_pairs={{0,4},{4,0},{8,12},{12,8},{16,20},{20,16},{24,28},{28,24},{1,5},{5... | collective-permute-start | bytes 1572872 | tf_op jit(solution)/shard_map/ppermute | solution.py:249
  24.3 58.3 %collective-permute-start.7 = (bf16[4,256,256]{2,1,0:T(8,128)(2,1)}, bf16[4,256,256]{2,1,0:T(8,128)(2,1)}, u32[]{:S(2)}, u32[]{:S(2)}) collective-permute-start(bf16[4,256,256]{2,1,0:T(8,128)(2,1)} %get-tuple-element.36), channel_id=1, source_target_pairs={{0,8},{4,12},{8,0},{12,4},{16,24},{20,28},{24,16},{28,20},{1,9},{5... | collective-permute-start | bytes 1572872 | tf_op jit(solution)/shard_map/ppermute | solution.py:249
  25.9 56.9 %collective-permute-start.5 = (bf16[4,256,256]{2,1,0:T(8,128)(2,1)S(1)}, bf16[4,256,256]{2,1,0:T(8,128)(2,1)S(1)}, u32[]{:S(2)}, u32[]{:S(2)}) collective-permute-start(bf16[4,256,256]{2,1,0:T(8,128)(2,1)S(1)} %pad_maximum_fusion.rest_0_), channel_id=1, source_target_pairs={{0,12},{4,8},{8,4},{12,0},{1,13},{5,9},{9,5},{13,1},{2,14},{6,10},... | collective-permute-start | bytes 1572872 | tf_op jit(solution)/shard_map/ppermute | solution.py:412
  27.4 56.3 %collective-permute-start.4 = (bf16[4,256,256]{2,1,0:T(8,128)(2,1)S(1)}, bf16[4,256,256]{2,1,0:T(8,128)(2,1)S(1)}, u32[]{:S(2)}, u32[]{:S(2)}) collective-permute-start(bf16[4,256,256]{2,1,0:T(8,128)(2,1)S(1)} %pad_maximum_fusion.rest_0_), channel_id=1, source_target_pairs={{0,8},{4,12},{8,0},{12,4},{1,9},{5,13},{9,1},{13,5},{2,10},{6,14},... | collective-permute-start | bytes 1572872 | tf_op jit(solution)/shard_map/ppermute | solution.py:412
  27.9 56.7 %collective-permute-start.3 = (bf16[4,256,256]{2,1,0:T(8,128)(2,1)S(1)}, bf16[4,256,256]{2,1,0:T(8,128)(2,1)S(1)}, u32[]{:S(2)}, u32[]{:S(2)}) collective-permute-start(bf16[4,256,256]{2,1,0:T(8,128)(2,1)S(1)} %pad_maximum_fusion.rest_0_), channel_id=1, source_target_pairs={{0,4},{4,0},{8,12},{12,8},{1,5},{5,1},{9,13},{13,9},{2,6},{6,2},{1... | collective-permute-start | bytes 1572872 | tf_op jit(solution)/shard_map/ppermute | solution.py:412
  81.2 151.3 %copy-start.9 = (s32[2]{0:T(128)}, s32[2]{0:T(128)S(1)}, u32[]{:S(2)}) copy-start(s32[2]{0:T(128)S(1)} %pad_add_fusion.3.spot) | copy-start | bytes 28
  81.2 57.9 %collective-permute-start.8 = (bf16[4,256,256]{2,1,0:T(8,128)(2,1)S(1)}, bf16[4,256,256]{2,1,0:T(8,128)(2,1)S(1)}, u32[]{:S(2)}, u32[]{:S(2)}) collective-permute-start(bf16[4,256,256]{2,1,0:T(8,128)(2,1)S(1)} %copy-done.8), channel_id=1, source_target_pairs={{0,12},{4,8},{8,4},{12,0},{16,28},{20,24},{24,20},{28,16},{1,13},{... | collective-permute-start | bytes 1572872 | tf_op jit(solution)/shard_map/ppermute | solution.py:249
  82.6 56.6 %collective-permute-start.9 = (bf16[4,256,256]{2,1,0:T(8,128)(2,1)S(1)}, bf16[4,256,256]{2,1,0:T(8,128)(2,1)S(1)}, u32[]{:S(2)}, u32[]{:S(2)}) collective-permute-start(bf16[4,256,256]{2,1,0:T(8,128)(2,1)S(1)} %copy-done.6), channel_id=1, source_target_pairs={{0,16},{4,20},{8,24},{12,28},{16,0},{20,4},{24,8},{28,12},{1,17},{... | collective-permute-start | bytes 1572872 | tf_op jit(solution)/shard_map/ppermute | solution.py:249
  82.7 56.4 %collective-permute-start.10 = (bf16[4,256,256]{2,1,0:T(8,128)(2,1)S(1)}, bf16[4,256,256]{2,1,0:T(8,128)(2,1)S(1)}, u32[]{:S(2)}, u32[]{:S(2)}) collective-permute-start(bf16[4,256,256]{2,1,0:T(8,128)(2,1)S(1)} %copy-done.4), channel_id=1, source_target_pairs={{0,20},{4,16},{8,28},{12,24},{16,4},{20,0},{24,12},{28,8},{1,21},{... | collective-permute-start | bytes 1572872 | tf_op jit(solution)/shard_map/ppermute | solution.py:249
  83.7 55.4 %collective-permute-start.11 = (bf16[4,256,256]{2,1,0:T(8,128)(2,1)S(1)}, bf16[4,256,256]{2,1,0:T(8,128)(2,1)S(1)}, u32[]{:S(2)}, u32[]{:S(2)}) collective-permute-start(bf16[4,256,256]{2,1,0:T(8,128)(2,1)S(1)} %copy-done.2), channel_id=1, source_target_pairs={{0,24},{4,28},{8,16},{12,20},{16,8},{20,12},{24,0},{28,4},{1,25},{... | collective-permute-start | bytes 1572872 | tf_op jit(solution)/shard_map/ppermute | solution.py:249
  84.6 54.6 %copy-start.11 = (bf16[4,256,256]{2,1,0:T(8,128)(2,1)S(1)}, bf16[4,256,256]{2,1,0:T(8,128)(2,1)}, u32[]{:S(2)}) copy-start(bf16[4,256,256]{2,1,0:T(8,128)(2,1)} %copy-done.10) | copy-start | bytes 1572868
  84.6 54.6 %collective-permute-start.12 = (bf16[4,256,256]{2,1,0:T(8,128)(2,1)S(1)}, bf16[4,256,256]{2,1,0:T(8,128)(2,1)S(1)}, u32[]{:S(2)}, u32[]{:S(2)}) collective-permute-start(bf16[4,256,256]{2,1,0:T(8,128)(2,1)S(1)} %get-tuple-element.41), channel_id=1, source_target_pairs={{0,28},{4,24},{8,20},{12,16},{16,12},{20,8},{24,4},{28,0},{1,29},{... | collective-permute-start | bytes 1572872 | tf_op jit(solution)/shard_map/ppermute | solution.py:249
  151.0 81.5 %copy-start.14 = (f32[512,512]{1,0:T(8,128)S(1)}, f32[512,512]{1,0:T(8,128)}, u32[]{:S(2)}) copy-start(f32[512,512]{1,0:T(8,128)} %copy-done.13) | copy-start | bytes 3145732
  151.0 81.5 %copy-start.16 = (f32[512,512]{1,0:T(8,128)S(1)}, f32[512,512]{1,0:T(8,128)}, u32[]{:S(2)}) copy-start(f32[512,512]{1,0:T(8,128)} %copy-done.15) | copy-start | bytes 3145732
  153.0 7.6 %collective-permute-start.16 = (s16[1296,256]{1,0:T(8,128)(2,1)S(1)}, s16[1296,256]{1,0:T(8,128)(2,1)S(1)}, u32[]{:S(2)}, u32[]{:S(2)}) collective-permute-start(s16[1296,256]{1,0:T(8,128)(2,1)S(1)} %get-tuple-element.62), channel_id=1, source_target_pairs={{0,0},{1,4},{2,8},{3,12},{4,1},{5,5},{6,9},{7,13},{8,2},{9,6},{10,... | collective-permute-start | bytes 1990664 | tf_op jit(solution)/shard_map/ppermute | solution.py:437
  153.7 77.0 %collective-permute-start.15 = (s16[1296,256]{1,0:T(8,128)(2,1)S(1)}, s16[1296,256]{1,0:T(8,128)(2,1)S(1)}, u32[]{:S(2)}, u32[]{:S(2)}) collective-permute-start(s16[1296,256]{1,0:T(8,128)(2,1)S(1)} %get-tuple-element.62), channel_id=1, source_target_pairs={{0,3},{1,2},{2,1},{3,0},{4,7},{5,6},{6,5},{7,4},{8,11},{9,10},{10,... | collective-permute-start | bytes 1990664 | tf_op jit(solution)/shard_map/ppermute | solution.py:412
  158.1 137.4 %collective-permute-start.14 = (s16[1296,256]{1,0:T(8,128)(2,1)S(1)}, s16[1296,256]{1,0:T(8,128)(2,1)S(1)}, u32[]{:S(2)}, u32[]{:S(2)}) collective-permute-start(s16[1296,256]{1,0:T(8,128)(2,1)S(1)} %get-tuple-element.62), channel_id=1, source_target_pairs={{0,2},{1,3},{2,0},{3,1},{4,6},{5,7},{6,4},{7,5},{8,10},{9,11},{10,... | collective-permute-start | bytes 1990664 | tf_op jit(solution)/shard_map/ppermute | solution.py:412
  160.0 135.5 %collective-permute-start.13 = (s16[1296,256]{1,0:T(8,128)(2,1)S(1)}, s16[1296,256]{1,0:T(8,128)(2,1)S(1)}, u32[]{:S(2)}, u32[]{:S(2)}) collective-permute-start(s16[1296,256]{1,0:T(8,128)(2,1)S(1)} %get-tuple-element.62), channel_id=1, source_target_pairs={{0,1},{1,0},{2,3},{3,2},{4,5},{5,4},{6,7},{7,6},{8,9},{9,8},{10,11... | collective-permute-start | bytes 1990664 | tf_op jit(solution)/shard_map/ppermute | solution.py:412
  160.6 136.3 %collective-permute-start.19 = (s16[1296,256]{1,0:T(8,128)(2,1)S(1)}, s16[1296,256]{1,0:T(8,128)(2,1)S(1)}, u32[]{:S(2)}, u32[]{:S(2)}) collective-permute-start(s16[1296,256]{1,0:T(8,128)(2,1)S(1)} %collective-permute-done.16), channel_id=1, source_target_pairs={{0,12},{4,8},{8,4},{12,0},{1,13},{5,9},{9,5},{13,1},{2,14},{6,10},... | collective-permute-start | bytes 1990664 | tf_op jit(solution)/shard_map/ppermute | solution.py:412
  218.9 78.0 %collective-permute-start.18 = (s16[1296,256]{1,0:T(8,128)(2,1)S(1)}, s16[1296,256]{1,0:T(8,128)(2,1)S(1)}, u32[]{:S(2)}, u32[]{:S(2)}) collective-permute-start(s16[1296,256]{1,0:T(8,128)(2,1)S(1)} %collective-permute-done.16), channel_id=1, source_target_pairs={{0,8},{4,12},{8,0},{12,4},{1,9},{5,13},{9,1},{13,5},{2,10},{6,14},... | collective-permute-start | bytes 1990664 | tf_op jit(solution)/shard_map/ppermute | solution.py:412
  230.7 66.1 %collective-permute-start.17 = (s16[1296,256]{1,0:T(8,128)(2,1)S(1)}, s16[1296,256]{1,0:T(8,128)(2,1)S(1)}, u32[]{:S(2)}, u32[]{:S(2)}) collective-permute-start(s16[1296,256]{1,0:T(8,128)(2,1)S(1)} %collective-permute-done.16), channel_id=1, source_target_pairs={{0,4},{4,0},{8,12},{12,8},{1,5},{5,1},{9,13},{13,9},{2,6},{6,2},{1... | collective-permute-start | bytes 1990664 | tf_op jit(solution)/shard_map/ppermute | solution.py:412
  (15 other events, 72.7 us)
